TPU v7x, 32 devices: a whole 2x2x4 slice. The times are simulated.
32 devices in a mesh: dp: 8 (over z, core), frame: 4 (over y, x).
Axes of the slice: x: 2, y: 2, z: 4, core: 2. Of those that a mesh axis runs over, the one named last changes fastest.
Arguments:
- latents: bfloat16 [8, 8, 128, 1280], P('dp', 'frame'), may hold values from -330 to 330
- timestep: int32 [8], P('dp'), may hold values from 0 to 999
- norm_gain: float32 [1280], replicated, may hold values from 0.1 to 1.9
- time_weight: bfloat16 [320, 1280], P('dp'), may hold values from -0.3125 to 0.3125
- conv_weight: bfloat16 [3, 1280, 1280], P(None, ('dp', 'frame')), may hold values from -0.09375 to 0.09375
- attend_weight: bfloat16 [1280, 3840], P(('dp', 'frame')), may hold values from -0.3354102 to 0.3354102
- output_weight: bfloat16 [1280, 1280], P(('dp', 'frame')), may hold values from -0.15625 to 0.15625
Outputs:
- block_out: bfloat16 [8, 8, 128, 1280], P('dp', 'frame')
All inputs are finite; a program needn't handle non-finite values.
Results may differ from a plain program's by a relative error of at most 0.0051.
Values may be sent and summed in bfloat16 or wider, within the bound.
A program may use at most 128 MiB of HBM per device.

v0:
```python
import math

import jax
import jax.numpy as jnp
from jax import lax
from jax.sharding import PartitionSpec as P

HEADS = 20
HD = 64
GROUPS = 32
TEMB = 320


def with_halo(array, sides, width):
    for axis, dim in sides:
        count, length = (lax.axis_size(axis), array.shape[dim])
        up = [(i, (i + 1) % count) for i in range(count - 1)]
        down = [(j, i) for i, j in up]
        last = lax.slice_in_dim(array, length - width, length, axis=dim)
        initial = lax.slice_in_dim(array, 0, width, axis=dim)
        before = lax.ppermute(last, axis, up)
        after = lax.ppermute(initial, axis, down)
        array = jnp.concatenate([before, array, after], axis=dim)
    return array


def sinusoid(timestep):
    half_dim = TEMB // 2
    ladder = jnp.arange(half_dim, dtype=jnp.float32)
    freqs = jnp.exp(-math.log(10000.0) * ladder / half_dim)
    angles = timestep.astype(jnp.float32)[:, None] * freqs[None, :]
    return jnp.concatenate([jnp.cos(angles), jnp.sin(angles)], axis=-1)


def attend_pixels(triple):
    count_items, frames_all, pixels_here, width_three = triple.shape
    channels = width_three // 3
    parts = triple.reshape(count_items, frames_all, pixels_here, 3, HEADS, HD)
    queries = parts[:, :, :, 0]
    key_part = parts[:, :, :, 1]
    value_part = parts[:, :, :, 2]
    scores = jnp.einsum(
        "nfphd,ngphd->nphfg", queries, key_part, preferred_element_type=jnp.float32
    ) / math.sqrt(HD)
    peak = jnp.max(scores, axis=-1, keepdims=True)
    expo = jnp.exp(scores - peak)
    probs = (expo / jnp.sum(expo, axis=-1, keepdims=True)).astype(jnp.bfloat16)
    attended = jnp.einsum(
        "nphfg,ngphd->nfphd", probs, value_part, preferred_element_type=jnp.float32
    )
    attended = attended.astype(jnp.bfloat16).reshape(count_items, frames_all, pixels_here, channels)
    return lax.all_to_all(attended, "frame", split_axis=1, concat_axis=2, tiled=True)


def shards(latents, timestep, norm_gain, time_weight, conv_weight, attend_weight, output_weight):
    count_clips, frames_dev, pixels, channels = latents.shape
    group_width = channels // GROUPS
    time_full = lax.all_gather(time_weight, "dp", axis=0, tiled=True)
    features = sinusoid(timestep).astype(jnp.bfloat16)
    time_bias = jnp.dot(features, time_full, preferred_element_type=jnp.float32)
    conv_full, attend_full, output_full = (
        lax.all_gather(conv_weight, ("dp", "frame"), axis=1, tiled=True),
        lax.all_gather(attend_weight, ("dp", "frame"), axis=0, tiled=True),
        lax.all_gather(output_weight, ("dp", "frame"), axis=0, tiled=True),
    )
    values = latents.astype(jnp.float32)
    grouped = values.reshape(count_clips, frames_dev, pixels, GROUPS, group_width)
    members = frames_dev * lax.axis_size("frame") * pixels * group_width
    center = lax.psum(jnp.sum(grouped, axis=(1, 2, 4)), "frame") / members
    deviate = grouped - center[:, None, None, :, None]
    spread = lax.psum(jnp.sum(deviate * deviate, axis=(1, 2, 4)), "frame") / members
    normed_group = deviate / jnp.sqrt(spread[:, None, None, :, None] + 1e-05)
    scaled = normed_group.reshape(count_clips, frames_dev, pixels, channels) * norm_gain
    hidden = jax.nn.silu(scaled).astype(jnp.bfloat16)
    padded = with_halo(hidden, (("frame", 1),), 1)
    windows = [padded[:, offset : offset + frames_dev].reshape(-1, channels) for offset in range(3)]
    conv_init = jnp.zeros((count_clips * frames_dev * pixels, channels), jnp.float32)
    conv = conv_init
    for offset in range(3):
        conv = conv + jnp.dot(
            windows[offset], conv_full[offset], preferred_element_type=jnp.float32
        )
    conv = conv.reshape(count_clips, frames_dev, pixels, channels) + time_bias[:, None, None, :]
    residual = (values + conv).astype(jnp.bfloat16)
    rows = residual.astype(jnp.float32)
    row_mean = jnp.mean(rows, axis=-1, keepdims=True)
    row_var = jnp.mean((rows - row_mean) ** 2, axis=-1, keepdims=True)
    normed = ((rows - row_mean) / jnp.sqrt(row_var + 1e-05)).astype(jnp.bfloat16)
    product = jnp.dot(normed.reshape(-1, channels), attend_full, preferred_element_type=jnp.float32)
    triple = product.astype(jnp.bfloat16).reshape(count_clips, frames_dev, pixels, 3 * channels)
    attended = attend_pixels(
        lax.all_to_all(triple, "frame", split_axis=2, concat_axis=1, tiled=True)
    )
    flat_attended = attended.reshape(-1, channels)
    projected = jnp.dot(flat_attended, output_full, preferred_element_type=jnp.float32)
    mixed = rows + projected.reshape(count_clips, frames_dev, pixels, channels)
    return mixed.astype(jnp.bfloat16)


def solution(mesh):
    in_specs = (
        P("dp", "frame", None, None),
        P("dp"),
        P(),
        P("dp", None),
        P(None, ("dp", "frame"), None),
        P(("dp", "frame"), None),
        P(("dp", "frame"), None),
    )
    out_specs = P("dp", "frame", None, None)
    return jax.shard_map(shards, mesh=mesh, in_specs=in_specs, out_specs=out_specs, check_vma=False)
```

profile of v0, /device:TPU:0, one launch (start us, length us, event | category | flops | bytes accessed | tf_op | source)
XLA Modules:
  0.0 276.7 jit_solution(11622464880846992532)
XLA Ops:
  6.5 0.7 all-gather.4.cloned.1.call-update
  7.3 0.7 all-gather.6.cloned.1.call-update
  8.1 1.2 convert_reduce_fusion.1
  9.5 11.4 %psum.14 = f32[1,32]{1,0:T(1,128)S(1)} all-reduce(f32[1,32]{1,0:T(1,128)S(1)} %bitcast.83), channel_id=1, replica_groups=mesh['dp'=8,'frame'=4] {'frame'}, use_global_device_ids=true, to_apply=%region_2.0 | all-reduce | flops 32 | bytes 256 | tf_op jit(solution)/shard_map/psum | solution.py:69
  21.0 0.2 fusion.27
  21.4 8.1 %psum.15 = f32[1,32]{1,0:T(1,128)S(1)} all-reduce(f32[1,32]{1,0:T(1,128)S(1)} %bitcast.82), channel_id=1, replica_groups=mesh['dp'=8,'frame'=4] {'frame'}, use_global_device_ids=true, to_apply=%region_5.6 | all-reduce | flops 32 | bytes 256 | tf_op jit(solution)/shard_map/psum | solution.py:71
  29.7 0.4 multiply_convert_fusion
  30.2 3.3 %collective-permute-start = (bf16[1,1,128,1280]{3,2,1,0:T(8,128)(2,1)S(1)}, bf16[1,1,128,1280]{3,2,1,0:T(8,128)(2,1)S(1)}, u32[]{:S(2)}, u32[]{:S(2)}) collective-permute-start(bf16[1,1,128,1280]{3,2,1,0:T(8,128)(2,1)S(1)} %get-tuple-element.12), channel_id=1, source_target_pairs={{0,1},{1,2},{2,3},{4,5},{5,6},{6,7},{8,9},{9,10},{10,11},{12,13},{... | collective-permute-start | bytes 983048 | tf_op jit(solution)/shard_map/ppermute | solution.py:21
  33.5 1.3 collective-permute-start.1
  35.5 20.3 %all_gather.13 = bf16[320,1280]{1,0:T(8,128)(2,1)S(1)} all-gather(bf16[40,1280]{1,0:T(8,128)(2,1)S(1)} %copy-done.1), channel_id=1, replica_groups=mesh['dp'=8,'frame'=4] {'dp'}, dimensions={0}, use_global_device_ids=true | all-gather | bytes 921600 | tf_op jit(solution)/shard_map/all_gather | solution.py:58
  55.9 0.2 convolution_reduce_fusion
  56.3 43.6 %all-gather.4.cloned.1.call-done = bf16[3,1280,1280]{2,1,0:T(8,128)(2,1)} async-done(((bf16[3,40,1280]{2,1,0:T(8,128)(2,1)}), bf16[3,1280,1280]{2,1,0:T(8,128)(2,1)}) %all-gather.4.cloned.1.call-update) | async-done | bytes 9830416 | tf_op jit(solution)/shard_map/all_gather | solution.py:62
  99.9 2.9 %fusion.1 = f32[256,1280]{1,0:T(8,128)S(1)} fusion(bf16[256,1280]{1,0:T(8,128)(2,1)S(1)} %bitcast.79, bf16[3,1280,1280]{2,1,0:T(8,128)(2,1)} %all-gather.4.cloned.1.call-done), kind=kOutput, calls=%fused_computation.3 | convolution fusion | flops 838860800 | bytes 5242880 | tf_op jit(solution)/shard_map/dot_general | solution.py:80
  102.8 2.9 %fusion.2 = f32[256,1280]{1,0:T(8,128)S(1)} fusion(bf16[256,1280]{1,0:T(8,128)(2,1)S(1)} %bitcast.73, bf16[3,1280,1280]{2,1,0:T(8,128)(2,1)} %all-gather.4.cloned.1.call-done), kind=kOutput, calls=%fused_computation.5 | convolution fusion | flops 838860800 | bytes 5242880 | tf_op jit(solution)/shard_map/dot_general | solution.py:80
  105.8 3.0 %fusion.7 = f32[256,1280]{1,0:T(8,128)S(1)} fusion(f32[256,1280]{1,0:T(8,128)S(1)} %fusion.1, f32[256,1280]{1,0:T(8,128)S(1)} %fusion.2, bf16[256,1280]{1,0:T(8,128)(2,1)S(1)} %bitcast.77, bf16[3,1280,1280]{2,1,0:T(8,128)(2,1)} %all-gather.4.cloned.1.call-done), kind=kOutput, calls=%fused_computation.11 | convolution fusion | flops 839516160 | bytes 7864320 | tf_op jit(solution)/shard_map/dot_general | solution.py:80
  108.8 0.3 convert_reduce_fusion
  109.1 0.3 fusion.25
  109.4 0.2 fusion.26
  109.6 75.5 %all-gather.6.cloned.1.call-done = bf16[1280,3840]{1,0:T(8,128)(2,1)} async-done(((bf16[40,3840]{1,0:T(8,128)(2,1)}), bf16[1280,3840]{1,0:T(8,128)(2,1)}) %all-gather.6.cloned.1.call-update) | async-done | bytes 9830416 | tf_op jit(solution)/shard_map/all_gather | solution.py:63
  185.2 6.5 %convolution_convert_fusion = bf16[256,3840]{1,0:T(8,128)(2,1)S(1)} fusion(bf16[256,1280]{1,0:T(8,128)(2,1)S(1)} %bitcast.80, bf16[1280,3840]{1,0:T(8,128)(2,1)} %all-gather.6.cloned.1.call-done), kind=kOutput, calls=%fused_computation.1 | convolution fusion | flops 2517565440 | bytes 12451840 | tf_op jit(solution)/shard_map/dot_general | solution.py:89
  191.7 2.0 copy.32
  193.7 30.0 %all_to_all.30 = bf16[1,2,128,3840]{3,1,0,2:T(2,128)(2,1)S(1)} all-to-all(bf16[1,2,128,3840]{3,1,0,2:T(2,128)(2,1)S(1)} %copy.32), channel_id=1, replica_groups=mesh['dp'=8,'frame'=4] {'frame'}, dimensions={2} | all-to-all | bytes 3932160 | tf_op jit(solution)/shard_map/all_to_all | solution.py:92
  223.7 0.2 copy.33
  224.1 4.5 %reshape.176 = bf16[1,8,32,3,20,64]{5,4,3,2,1,0:T(8,128)(2,1)} reshape(bf16[1,4,2,32,3840]{4,3,2,1,0:T(8,128)(2,1)S(1)} %copy.34) | data formatting | bytes 3932160 | tf_op jit(solution)/shard_map/reshape | solution.py:38
  228.5 3.2 %fusion.35 = (bf16[1,8,32,1,20,64]{5,4,3,2,1,0:T(8,128)(2,1)S(1)}, bf16[1,8,32,1,20,64]{5,4,3,2,1,0:T(8,128)(2,1)S(1)}, bf16[1,8,32,1,20,64]{5,4,3,2,1,0:T(8,128)(2,1)S(1)}) fusion(bf16[1,8,32,3,20,64]{5,4,3,2,1,0:T(8,128)(2,1)} %reshape.176), kind=kLoop, calls=%fused_computation.54 | loop fusion | bytes 3932160 | tf_op jit(solution)/shard_map/slice | solution.py:41
  231.8 1.6 fusion.30
  233.4 18.7 %fusion.37 = (f32[32,20,8]{2,1,0:T(8,128)S(1)}, f32[32,20,8,8]{2,3,1,0:T(8,128)S(1)}) fusion(f32[32,20,8,8]{2,3,1,0:T(8,128)S(1)} %fusion.30), kind=kOutput, calls=%fused_computation.56 | output fusion | flops 163847 | bytes 348160 | tf_op jit(solution)/shard_map/sub | solution.py:46
  252.1 1.2 fusion.24
  253.3 0.2 copy.39
  253.6 0.9 reshape.180
  254.5 11.8 %all_to_all.31 = bf16[1,8,32,1280]{3,2,0,1:T(8,128)(2,1)S(1)} all-to-all(bf16[1,8,32,1280]{3,2,0,1:T(8,128)(2,1)S(1)} %bitcast.76), channel_id=1, replica_groups=mesh['dp'=8,'frame'=4] {'frame'}, dimensions={1} | all-to-all | bytes 1310720 | tf_op jit(solution)/shard_map/all_to_all | solution.py:52
  266.4 3.8 %fusion.14 = bf16[1,2,128,1280]{3,2,1,0:T(8,128)(2,1)} fusion(bf16[2,128,1280]{2,1,0:T(8,128)(2,1)S(1)} %bitcast.81, bf16[1280,1280]{1,0:T(8,128)(2,1)} %all-gather.8.cloned.1.call-done, bf16[1,2,128,1280]{3,2,1,0:T(8,128)(2,1)S(1)} %get-tuple-element.6), kind=kOutput, calls=%fused_computation.16 | convolution fusion | flops 839843840 | bytes 5242880 | tf_op jit(solution)/shard_map/dot_general | solution.py:95
  (32 shorter events, 1.3 us)
Async XLA Ops:
  6.5 14.5 %copy-start = (bf16[1,2,128,1280]{3,2,1,0:T(8,128)(2,1)S(1)}, bf16[1,2,128,1280]{3,2,1,0:T(8,128)(2,1)}, u32[]{:S(2)}) copy-start(bf16[1,2,128,1280]{3,2,1,0:T(8,128)(2,1)} %param.7) | copy-start | bytes 1966084
  6.5 23.2 %copy-start.2 = (f32[1280]{0:T(1024)S(1)}, f32[1280]{0:T(1024)}, u32[]{:S(2)}) copy-start(f32[1280]{0:T(1024)} %param.9) | copy-start | bytes 15364
  6.5 93.3 %all-gather.4.cloned.1.call-start = ((), (), s32[]{:S(2)}) async-start(), calls=%async_computation.2 | async-start | bytes 10137600 | tf_op jit(solution)/shard_map/all_gather | solution.py:62
  7.3 177.9 %all-gather.6.cloned.1.call-start = ((), (), s32[]{:S(2)}) async-start(), calls=%async_computation.3 | async-start | bytes 10137600 | tf_op jit(solution)/shard_map/all_gather | solution.py:63
  8.0 258.3 %all-gather.8.cloned.1.call-start = ((), (), s32[]{:S(2)}) async-start(), calls=%async_computation.4 | async-start | bytes 3379200 | tf_op jit(solution)/shard_map/all_gather | solution.py:64
  21.2 14.3 %copy-start.1 = (bf16[40,1280]{1,0:T(8,128)(2,1)S(1)}, bf16[40,1280]{1,0:T(8,128)(2,1)}, u32[]{:S(2)}) copy-start(bf16[40,1280]{1,0:T(8,128)(2,1)} %param.10) | copy-start | bytes 307204
  30.2 26.0 %collective-permute-start = (bf16[1,1,128,1280]{3,2,1,0:T(8,128)(2,1)S(1)}, bf16[1,1,128,1280]{3,2,1,0:T(8,128)(2,1)S(1)}, u32[]{:S(2)}, u32[]{:S(2)}) collective-permute-start(bf16[1,1,128,1280]{3,2,1,0:T(8,128)(2,1)S(1)} %get-tuple-element.12), channel_id=1, source_target_pairs={{0,1},{1,2},{2,3},{4,5},{5,6},{6,7},{8,9},{9,10},{10,11},{12,13},{... | collective-permute-start | bytes 983048 | tf_op jit(solution)/shard_map/ppermute | solution.py:21
  33.5 22.7 %collective-permute-start.1 = (bf16[1,1,128,1280]{3,2,1,0:T(8,128)(2,1)S(1)}, bf16[1,1,128,1280]{3,2,1,0:T(8,128)(2,1)S(1)}, u32[]{:S(2)}, u32[]{:S(2)}) collective-permute-start(bf16[1,1,128,1280]{3,2,1,0:T(8,128)(2,1)S(1)} %get-tuple-element.13), channel_id=1, source_target_pairs={{1,0},{2,1},{3,2},{5,4},{6,5},{7,6},{9,8},{10,9},{11,10},{13,12},{... | collective-permute-start | bytes 983048 | tf_op jit(solution)/shard_map/ppermute | solution.py:22
Sparse Core Ops, SparseCore 0:
  10.2 89.5 all-gather.3
  102.8 82.3 all-gather.5
  188.0 60.3 all-gather.7
where the time goes:
time: 277 us
  waiting for transfers between devices  121 us (44%)
  blocking collectives  81.6 us (29%)
  matrix products  22.2 us (8%)
  other arithmetic  21.9 us (8%)
  between operations  14 us (5%)
  local copies, waits for them, and re-layouts  11.8 us (4%)
  starting transfers between devices  4.66 us (2%)
    all_gather x1, waiting for transfers between devices, shards(): lax.all_gather(attend_weight, ('dp', 'frame'), axis=0, tiled=True)  75.5 us
    all_gather x1, waiting for transfers between devices, shards(): lax.all_gather(conv_weight, ('dp', 'frame'), axis=1, tiled=True)  43.6 us
    all_to_all x1, blocking collectives, shards(): lax.all_to_all(triple, 'frame', split_axis=2, concat_axis=1, tiled=True)  30 us
    all_gather x1, blocking collectives, shards(): time_full = lax.all_gather(time_weight, 'dp', axis=0, tiled=True)  20.3 us
    sub x1, other arithmetic, attend_pixels(): expo = jnp.exp(scores - peak)  18.7 us
    all_to_all x1, blocking collectives, attend_pixels(): lax.all_to_all(attended, 'frame', split_axis=1, concat_axis=2, tiled=True)  11.8 us
    psum x1, blocking collectives, shards(): center = lax.psum(jnp.sum(grouped, axis=(1, 2, 4)), 'frame') / members  11.4 us
    dot_general x3, matrix products, shards(): jnp.dot(windows[offset], conv_full[offset], preferred_element_type=jnp.fl...  8.88 us
  transfers between devices with their start and end apart: 5, of which 2 were waited for; matrix products, arithmetic and copies ran while one was open for 19% of the time, Pallas kernels for 0%

commit v1 on v0

--- a/solution.py
+++ b/solution.py
@@ -1,8 +1,12 @@
+import functools
 import math
 
 import jax
 import jax.numpy as jnp
+import numpy as np
 from jax import lax
+from jax.experimental import pallas as pl
+from jax.experimental.pallas import tpu as pltpu
 from jax.sharding import PartitionSpec as P
 
 HEADS = 20
@@ -97,6 +101,412 @@
     return mixed.astype(jnp.bfloat16)
 
 
+F32 = jnp.float32
+BF16 = jnp.bfloat16
+HPAD = 384
+
+
+def split_rows(row):
+    hi = row.astype(BF16).astype(F32)
+    mid = (row - hi).astype(BF16).astype(F32)
+    low = row - hi - mid
+    place = lax.broadcasted_iota(jnp.int32, (16, row.shape[1]), 0)
+    both = jnp.where(place == 0, hi, jnp.where(place == 1, mid, jnp.where(place == 2, low, 0.0)))
+    return both.astype(BF16)
+
+
+def group_mean(row, ind, ind_back, count):
+    sums = jnp.dot(split_rows(row), ind, preferred_element_type=F32)
+    sums = jnp.sum(sums, axis=0, keepdims=True) / count
+    wide = jnp.dot(split_rows(sums), ind_back, preferred_element_type=F32)
+    return jnp.sum(wide, axis=0, keepdims=True)
+
+
+def kernel(
+    planes, dps, lat_ref, feat_ref, gain_ref, time_ref, conv_ref, att_ref, outw_ref,
+    ind_ref, indb_ref, e_ref, et_ref, out_ref,
+    L, H, S1, S2, A1, A2, GC, GA, Y, RS, Q, K, V, ATS, AT, WO,
+    lat_s, lat_r, a_s, a_r, g_s, g_r, rs_s, rs_r, at_s, at_r, wo_s, wo_r, wf_s,
+):
+    d = lax.axis_index("dp")
+    f = lax.axis_index("frame")
+    z = d // 2
+    c = d % 2
+    sib = d + 1 - 2 * c
+    levels = dps // 2
+    frames, pixels, channels = L.shape
+    mine = frames // planes
+    cols = channels // planes
+    depth = conv_ref.shape[1]
+    block = planes * depth
+
+    barrier = pltpu.get_barrier_semaphore()
+    for j in range(1, planes):
+        pl.semaphore_signal(barrier, inc=1, device_id={"frame": lax.rem(f + j, planes)}, device_id_type=pl.DeviceIdType.MESH)
+    for j in range(1, dps):
+        pl.semaphore_signal(barrier, inc=1, device_id={"dp": lax.rem(d + j, dps)}, device_id_type=pl.DeviceIdType.MESH)
+
+    zeros8 = jnp.zeros((8, 3 * cols), F32)
+    zeros8b = jnp.zeros((8, 4 * cols), F32)
+    for j in range(planes):
+        part = slice(j * cols, (j + 1) * cols)
+        taps = [conv_ref[t].astype(F32)[:, part] for t in range(3)]
+        S1[j] = jnp.concatenate([jnp.concatenate(taps, axis=1), zeros8], axis=0).astype(BF16)
+        att = att_ref[...].astype(F32)
+        quads = [att[:, t * channels + j * cols : t * channels + (j + 1) * cols] for t in range(3)]
+        quads.append(outw_ref[...].astype(F32)[:, part])
+        S2[j] = jnp.concatenate([jnp.concatenate(quads, axis=1), zeros8b], axis=0).astype(BF16)
+    pl.semaphore_wait(barrier, planes - 1 + dps - 1)
+
+    def remote(src, dst, ss, rs, where):
+        return pltpu.make_async_remote_copy(
+            src_ref=src, dst_ref=dst, send_sem=ss, recv_sem=rs, device_id=where,
+            device_id_type=pl.DeviceIdType.MESH,
+        )
+
+    def peer(j):
+        return lax.rem(f + j, planes)
+
+    def source(j):
+        return lax.rem(f + planes - j, planes)
+
+    my_frames = pl.ds(f * mine, mine)
+
+    def a_copy(k, j):
+        src, dst = ((S1, A1), (S2, A2))[k]
+        p = peer(j)
+        return remote(src.at[p], dst.at[f], a_s.at[k, j], a_r.at[k, j], {"frame": p})
+
+    def lat_copy(j):
+        return remote(lat_ref, L.at[my_frames], lat_s.at[j], lat_r.at[j], {"frame": peer(j)})
+
+    for j in range(1, planes):
+        a_copy(0, j).start()
+    for j in range(1, planes):
+        lat_copy(j).start()
+    for j in range(1, planes):
+        a_copy(1, j).start()
+    L[my_frames] = lat_ref[...]
+    A1[f] = S1[f]
+    A2[f] = S2[f]
+
+    def stack(buf):
+        return jnp.concatenate([buf[j].astype(F32)[:depth] for j in range(planes)], axis=0)
+
+    G = (GC, GA)
+
+    def g_copy(k, owner, slot, target):
+        return remote(G[k].at[owner], G[k].at[owner], g_s.at[k, slot], g_r.at[k, owner], {"dp": target})
+
+    def guarded(cond, fn):
+        pl.when(cond)(fn)
+
+    def push(k, owner, step, right, left, act):
+        if right is not None:
+            guarded(right, lambda: act(g_copy(k, owner, 3 * step, d + 2)))
+        if left is not None:
+            guarded(left, lambda: act(g_copy(k, owner, 3 * step + 1, d - 2)))
+        return None
+
+    def steps_of(k, step, act):
+        if step == 0:
+            guarded(z < levels - 1, lambda: act(0, d, 0, d + 2))
+            guarded(z > 0, lambda: act(0, d, 1, d - 2))
+            act(0, d, 2, sib)
+            return
+        below = d - 2 * step
+        above = d + 2 * step
+        base = 4 * step - 1
+
+        @pl.when(z >= step)
+        def _():
+            act(1, below, 0, sib)
+            guarded(z < levels - 1, lambda: act(0, below, base, d + 2))
+            act(0, below, base + 1, sib)
+
+        @pl.when(z + step < levels)
+        def _():
+            act(1, above, 0, sib)
+            guarded(z > 0, lambda: act(0, above, base + 2, d - 2))
+            act(0, above, base + 3, sib)
+
+    def relay(k, step):
+        def act(kind, owner, slot, target):
+            copy = g_copy(k, owner, slot, target)
+            if kind == 1:
+                copy.wait_recv()
+            else:
+                copy.start()
+
+        steps_of(k, step, act)
+
+    def drain(k):
+        def act(kind, owner, slot, target):
+            if kind == 0:
+                g_copy(k, owner, slot, target).wait_send()
+
+        for step in range(levels):
+            steps_of(k, step, act)
+
+    def from_sibling(k):
+        for zz in range(levels):
+            g_copy(k, 2 * zz + 1 - c, 0, sib).wait_recv()
+
+    for j in range(1, planes):
+        a_copy(0, j).wait_recv()
+    GC[d, 0:block] = stack(A1).astype(BF16)
+    GC[d, block : block + 16] = time_ref[...]
+    relay(0, 0)
+    for j in range(1, planes):
+        a_copy(1, j).wait_recv()
+    GA[d] = stack(A2).astype(BF16)
+    for step in range(1, levels):
+        relay(0, step)
+    relay(1, 0)
+
+    for j in range(1, planes):
+        lat_copy(j).wait_recv()
+
+    def fold(rows):
+        return jnp.sum(rows.reshape(pixels // 8, 8, channels), axis=0)
+
+    def sum_frame(i, acc):
+        return acc + fold(L[i].astype(F32))
+
+    start = jnp.zeros((8, channels), F32)
+    total = lax.fori_loop(0, frames, sum_frame, start)
+    count = float(frames * pixels * (channels // GROUPS))
+    ind, indb = ind_ref[...], indb_ref[...]
+    center = group_mean(jnp.sum(total, axis=0, keepdims=True), ind, indb, count)
+
+    def dev_frame(i, acc):
+        dev = L[i].astype(F32) - center
+        return acc + fold(dev * dev)
+
+    total2 = lax.fori_loop(0, frames, dev_frame, start)
+    spread = group_mean(jnp.sum(total2, axis=0, keepdims=True), ind, indb, count)
+    scale = gain_ref[...] / jnp.sqrt(spread + 1e-05)
+
+    def hide_frame(i, carry):
+        scaled = (L[i].astype(F32) - center) * scale
+        H[i] = (scaled / (1.0 + jnp.exp(-scaled))).astype(BF16)
+        return carry
+
+    lax.fori_loop(0, frames, hide_frame, 0)
+    relay(1, 1)
+
+    from_sibling(0)
+    Y[0] = jnp.zeros(Y.shape[1:], F32)
+    Y[frames + 1] = jnp.zeros(Y.shape[1:], F32)
+
+    def conv_pair(i, carry):
+        rows = H[pl.ds(2 * i, 2)].reshape(2 * pixels, channels)
+        weight = GC[:, 0:block, :].reshape(dps * block, 3 * cols)
+        y = jnp.dot(rows, weight, preferred_element_type=F32)
+        Y[pl.ds(2 * i + 1, 2)] = y.reshape(2, pixels, 3 * cols)
+        return carry
+
+    lax.fori_loop(0, frames // 2, conv_pair, 0)
+    times = GC[:, block : block + 16, :].reshape(dps * 16, 3 * cols)
+    tb = jnp.dot(feat_ref[...], times, preferred_element_type=F32)
+    bias = tb[0:1, 0:cols] + tb[1:2, cols : 2 * cols] + tb[2:3, 2 * cols : 3 * cols]
+
+    def res_frame(i, carry):
+        conv = Y[i][:, 0:cols] + Y[i + 1][:, cols : 2 * cols] + Y[i + 2][:, 2 * cols : 3 * cols]
+        x = L[i].astype(F32)
+        own = x[:, 0:cols]
+        for j in range(1, planes):
+            own = jnp.where(f == j, x[:, j * cols : (j + 1) * cols], own)
+        RS[f, i] = (own + (conv + bias)).astype(BF16)
+        return carry
+
+    lax.fori_loop(0, frames, res_frame, 0)
+
+    def rs_copy(j):
+        return remote(RS.at[f], RS.at[f], rs_s.at[j], rs_r.at[j], {"frame": peer(j)})
+
+    for j in range(1, planes):
+        rs_copy(j).start()
+    for step in range(2, levels):
+        relay(1, step)
+    from_sibling(1)
+
+    half = dps * block // 2
+    WO[f] = GA[:, :, 3 * cols : 4 * cols].reshape(dps * block, cols)
+
+    def wo_copy(j):
+        part = pl.ds(pl.multiple_of(c * half, 16), half)
+        return remote(WO.at[f, part], WO.at[f, part], wo_s.at[j], wo_r.at[j, 0], {"frame": peer(j)})
+
+    def wo_share(j):
+        part = pl.ds(pl.multiple_of(c * half, 16), half)
+        s = source(j)
+        return remote(WO.at[s, part], WO.at[s, part], wf_s.at[j], wo_r.at[j, 1], {"dp": sib})
+
+    for j in range(1, planes):
+        rs_copy(j).wait_recv()
+    for j in range(1, planes):
+        wo_copy(j).start()
+
+    def rows_of(i):
+        return jnp.concatenate([RS[j, i].astype(F32) for j in range(planes)], axis=1)
+
+    def norm_frame(i, carry):
+        rows = rows_of(i)
+        mean = jnp.mean(rows, axis=-1, keepdims=True)
+        dev = rows - mean
+        var = jnp.mean(dev * dev, axis=-1, keepdims=True)
+        H[i] = (dev / jnp.sqrt(var + 1e-05)).astype(BF16)
+        return carry
+
+    lax.fori_loop(0, frames, norm_frame, 0)
+    pad = jnp.zeros((pixels, HPAD - cols), F32)
+
+    def triple_pair(i, carry):
+        rows = H[pl.ds(2 * i, 2)].reshape(2 * pixels, channels)
+        weight = GA[:, :, 0 : 3 * cols].reshape(dps * block, 3 * cols)
+        y = jnp.dot(rows, weight, preferred_element_type=F32)
+        for n in range(2):
+            for t, buf in enumerate((Q, K, V)):
+                piece = y[n * pixels : (n + 1) * pixels, t * cols : (t + 1) * cols]
+                buf[2 * i + n] = jnp.concatenate([piece, pad], axis=1).astype(BF16)
+        return carry
+
+    lax.fori_loop(0, frames // 2, triple_pair, 0)
+
+    def attend(i, carry):
+        q = Q[i]
+        prods = jnp.concatenate([q * K[g] for g in range(frames)], axis=1)
+        scores = jnp.dot(prods, e_ref[...], preferred_element_type=F32) * (1.0 / math.sqrt(HD))
+        peak = scores
+        for shift in (8, 16, 32):
+            peak = jnp.maximum(peak, pltpu.roll(peak, shift, 1))
+        expo = jnp.exp(scores - peak)
+        total = expo
+        for shift in (8, 16, 32):
+            total = total + pltpu.roll(total, shift, 1)
+        probs = (expo / total).astype(BF16)
+        spreads = jnp.dot(probs, et_ref[...], preferred_element_type=F32)
+        acc = spreads[:, 0:HPAD] * V[0].astype(F32)
+        for g in range(1, frames):
+            acc = acc + spreads[:, g * HPAD : (g + 1) * HPAD] * V[g].astype(F32)
+        ATS[i] = acc[:, 0:cols].astype(BF16)
+        return carry
+
+    lax.fori_loop(0, frames, attend, 0)
+
+    def at_copy(j):
+        p = peer(j)
+        return remote(ATS.at[pl.ds(p * mine, mine)], AT.at[f], at_s.at[j], at_r.at[j], {"frame": p})
+
+    for j in range(1, planes):
+        at_copy(j).start()
+    AT[f] = ATS[my_frames]
+    for j in range(1, planes):
+        wo_copy(j).wait_recv()
+        wo_share(j).start()
+    for j in range(1, planes):
+        wo_share(j).wait_recv()
+    for j in range(1, planes):
+        at_copy(j).wait_recv()
+
+    def out_frame(i, carry):
+        a = jnp.concatenate([AT[j, i].astype(F32) for j in range(planes)], axis=1).astype(BF16)
+        parts = [jnp.dot(a, WO[j], preferred_element_type=F32) for j in range(planes)]
+        mixed = rows_of(f * mine + i) + jnp.concatenate(parts, axis=1)
+        out_ref[i] = mixed.astype(BF16)
+        return carry
+
+    lax.fori_loop(0, mine, out_frame, 0)
+
+    for j in range(1, planes):
+        a_copy(0, j).wait_send()
+        a_copy(1, j).wait_send()
+        lat_copy(j).wait_send()
+        rs_copy(j).wait_send()
+        wo_copy(j).wait_send()
+        wo_share(j).wait_send()
+        at_copy(j).wait_send()
+    drain(0)
+    drain(1)
+
+
+def indicators(frames, channels, cols):
+    group = np.arange(channels) // (channels // GROUPS)
+    ind = (group[:, None] == np.arange(128)[None, :]).astype(np.float32)
+    row = np.arange(frames * HPAD)
+    item, head = row // HPAD, (row % HPAD) // HD
+    lane = np.arange(128)
+    hit = (item[:, None] == (lane % 64)[None, :] // 8) & (head[:, None] == lane[None, :] % 8)
+    hit = hit & (head < cols // HD)[:, None]
+    back = (hit & (lane < 64)[None, :]).T
+    return [jnp.asarray(m, BF16) for m in (ind, ind.T, hit.astype(np.float32), back.astype(np.float32))]
+
+
+def fast_shards(latents, timestep, norm_gain, time_weight, conv_weight, attend_weight, output_weight):
+    planes, dps = lax.axis_size("frame"), lax.axis_size("dp")
+    _, mine, pixels, channels = latents.shape
+    frames = mine * planes
+    cols = channels // planes
+    depth = conv_weight.shape[1]
+    block = depth * planes
+    f = lax.axis_index("frame")
+    rows = time_weight.shape[0]
+    features = sinusoid(timestep).astype(BF16).reshape(dps, rows)
+    features = jnp.pad(features, ((0, 0), (0, 48 - rows))).reshape(dps, 3, 16)
+    feats = jnp.pad(features.transpose(1, 0, 2).reshape(3, dps * 16), ((0, 13), (0, 0)))
+    times = lax.dynamic_slice_in_dim(time_weight, f * cols, cols, axis=1)
+    times = jnp.pad(times, ((0, 48 - rows), (0, 0))).reshape(3, 16, cols)
+    times = times.transpose(1, 0, 2).reshape(16, 3 * cols)
+    ind, indb, e, et = indicators(frames, channels, cols)
+    vmem = pl.BlockSpec(memory_space=pltpu.VMEM)
+    DMA = pltpu.SemaphoreType.DMA
+    slots = 4 * (dps // 2)
+    out = pl.pallas_call(
+        functools.partial(kernel, planes, dps),
+        out_shape=jax.ShapeDtypeStruct((mine, pixels, channels), BF16),
+        in_specs=[vmem] * 11,
+        out_specs=vmem,
+        scratch_shapes=[
+            pltpu.VMEM((frames, pixels, channels), BF16),
+            pltpu.VMEM((frames, pixels, channels), BF16),
+            pltpu.VMEM((planes, depth + 8, 3 * cols), BF16),
+            pltpu.VMEM((planes, depth + 8, 4 * cols), BF16),
+            pltpu.VMEM((planes, depth + 8, 3 * cols), BF16),
+            pltpu.VMEM((planes, depth + 8, 4 * cols), BF16),
+            pltpu.VMEM((dps, block + 16, 3 * cols), BF16),
+            pltpu.VMEM((dps, block, 4 * cols), BF16),
+            pltpu.VMEM((frames + 2, pixels, 3 * cols), F32),
+            pltpu.VMEM((planes, frames, pixels, cols), BF16),
+            pltpu.VMEM((frames, pixels, HPAD), BF16),
+            pltpu.VMEM((frames, pixels, HPAD), BF16),
+            pltpu.VMEM((frames, pixels, HPAD), BF16),
+            pltpu.VMEM((frames, pixels, cols), BF16),
+            pltpu.VMEM((planes, mine, pixels, cols), BF16),
+            pltpu.VMEM((planes, dps * block, cols), BF16),
+            DMA((planes,)), DMA((planes,)),
+            DMA((2, planes)), DMA((2, planes)),
+            DMA((2, slots)), DMA((2, dps)),
+            DMA((planes,)), DMA((planes,)),
+            DMA((planes,)), DMA((planes,)),
+            DMA((planes,)), DMA((planes, 2)), DMA((planes,)),
+        ],
+        compiler_params=pltpu.CompilerParams(
+            collective_id=0, has_side_effects=True, vmem_limit_bytes=56 * 1024 * 1024
+        ),
+        cost_estimate=pl.CostEstimate(flops=7_000_000_000, bytes_accessed=8_000_000, transcendentals=3_000_000),
+    )(
+        latents[0], feats, norm_gain[None, :], times, conv_weight, attend_weight, output_weight,
+        ind, indb, e, et,
+    )
+    return out[None]
+
+
+def fits(mesh):
+    planes, dps = mesh.shape["frame"], mesh.shape["dp"]
+    return planes == 4 and dps == 8
+
+
 def solution(mesh):
     in_specs = (
         P("dp", "frame", None, None),
@@ -108,4 +518,4 @@
         P(("dp", "frame"), None),
     )
     out_specs = P("dp", "frame", None, None)
-    return jax.shard_map(shards, mesh=mesh, in_specs=in_specs, out_specs=out_specs, check_vma=False)
+    return jax.shard_map(fast_shards if fits(mesh) else shards, mesh=mesh, in_specs=in_specs, out_specs=out_specs, check_vma=False)

time: 277 us -> 154 us (0.56)
  Pallas kernels: 0 us -> 148 us
  waiting for transfers between devices: 121 us -> 0 us
  blocking collectives: 81.6 us -> 0 us
  matrix products: 22.2 us -> 0 us
  other arithmetic: 21.9 us -> 0.15 us
  between operations: 14 us -> 0.73 us
  local copies, waits for them, and re-layouts: 11.8 us -> 4.69 us
  starting transfers between devices: 4.66 us -> 0 us
    pallas_call x0 -> x1, Pallas kernels: none -> 148 us  [fast_shards(): pl.pallas_call(functools.partial(kernel, planes, dps), out_shape=jax.Shap...]
    all_gather x3 -> x0, waiting for transfers between devices: 119 us -> none  [the longest x1 75.5 us: shards(): lax.all_gather(attend_weight, ('dp', 'frame'), axis=0, tiled=True)]
    all_to_all x2 -> x0, blocking collectives: 41.8 us -> none  [the longest x1 30 us: shards(): lax.all_to_all(triple, 'frame', split_axis=2, concat_axis=1, tiled=True)]
    dot_general x8 -> x0, matrix products: 22.2 us -> none  [the longest x3 8.88 us: shards(): jnp.dot(windows[offset], conv_full[offset], preferred_element_type=jnp.fl...]
    all_gather x1 -> x0, blocking collectives: 20.3 us -> none  [shards(): time_full = lax.all_gather(time_weight, 'dp', axis=0, tiled=True)]
    psum x2 -> x0, blocking collectives: 19.5 us -> none  [the longest x1 11.4 us: shards(): center = lax.psum(jnp.sum(grouped, axis=(1, 2, 4)), 'frame') / members]
    sub x2 -> x0, other arithmetic: 18.7 us -> none  [the longest x1 18.7 us: attend_pixels(): expo = jnp.exp(scores - peak)]
    reshape x3 -> x4, local copies, waits for them, and re-layouts: 7.41 us -> 0.9 us  [the longest x1 0.71 us: fast_shards(): times = times.transpose(1, 0, 2).reshape(16, 3 * cols)]
  transfers between devices with their start and end apart: 5 -> 0, of which waited for: 2 -> 0; matrix products, arithmetic and copies ran while one was open for 19% -> 0% of each run, Pallas kernels for 0% -> 0%
where the time goes in v1:
time: 154 us; the launch traced here: 153 us
  Pallas kernels  148 us (96%)
  local copies, waits for them, and re-layouts  4.69 us (3%)
    pallas_call x1, Pallas kernels, fast_shards(): pl.pallas_call(functools.partial(kernel, planes, dps), out_shape=jax.Shap...  148 us

profile of v1, /device:TPU:0, one launch (start us, length us, event | category | flops | bytes accessed | tf_op | source)
XLA Modules:
  0.0 153.2 jit_solution(3228898442096092249)
XLA Ops:
  0.0 0.0 copy-start
  0.7 0.0 copy-start.1
  0.7 0.1 sine_convert_fusion
  0.8 0.1 maximum_reduce_fusion
  0.9 0.1 convert_element_type.17
  1.0 0.4 copy-done.1
  1.4 0.6 broadcast_in_dim.8.gain_ref
  2.0 0.1 reshape.42
  2.1 0.1 reshape.43
  2.2 0.6 pad.13.feat_ref
  2.8 0.0 copy-done
  2.8 0.1 constant_dynamic-slice_fusion
  2.9 0.7 reshape.45.time_ref
  3.6 147.6 %shard_map.109 = bf16[2,128,1280]{2,1,0:T(8,128)(2,1)} custom-call(bf16[2,128,1280]{2,1,0:T(8,128)(2,1)} %bitcast.12, bf16[16,128]{1,0:T(8,128)(2,1)} %pad.13.feat_ref, f32[1,1280]{1,0:T(1,128)} %broadcast_in_dim.8.gain_ref, bf16[16,960]{1,0:T(8,128)(2,1)} %reshape.45.time_ref, bf16[3,40,1280]{2,1,0:T(8,128)(2,1)} %conv_ref.1, bf16[40,3840]{1,0:T(8,128)(2,1)} %att_ref.1, ...), custom_call_target="tpu_custom_call" | custom-call | flops 7000000000 | bytes 8000000 | tf_op jit(solution)/shard_map/pallas_call | solution.py:465
  151.2 2.0 %copy.19 = bf16[1,2,128,1280]{3,2,1,0:T(8,128)(2,1)} copy(bf16[1,2,128,1280]{3,2,1,0:T(8,128)(2,1)} %bitcast.8) | data formatting | bytes 1310720
  (4 shorter events, 0.0 us)
Async XLA Ops:
  0.0 2.8 %copy-start = (bf16[40,1280]{1,0:T(8,128)(2,1)S(1)}, bf16[40,1280]{1,0:T(8,128)(2,1)}, u32[]{:S(2)}) copy-start(bf16[40,1280]{1,0:T(8,128)(2,1)} %param.14) | copy-start | bytes 307204
  0.7 0.7 copy-start.1

commit v2 on v1

--- a/solution.py
+++ b/solution.py
@@ -146,16 +146,16 @@
     for j in range(1, dps):
         pl.semaphore_signal(barrier, inc=1, device_id={"dp": lax.rem(d + j, dps)}, device_id_type=pl.DeviceIdType.MESH)
 
-    zeros8 = jnp.zeros((8, 3 * cols), F32)
-    zeros8b = jnp.zeros((8, 4 * cols), F32)
+    zeros3 = jnp.zeros((8, 3 * cols), F32)
+    zeros4 = jnp.zeros((8, 4 * cols), F32)
+    att = att_ref[...].astype(F32)
+    outw = outw_ref[...].astype(F32)
     for j in range(planes):
         part = slice(j * cols, (j + 1) * cols)
-        taps = [conv_ref[t].astype(F32)[:, part] for t in range(3)]
-        S1[j] = jnp.concatenate([jnp.concatenate(taps, axis=1), zeros8], axis=0).astype(BF16)
-        att = att_ref[...].astype(F32)
-        quads = [att[:, t * channels + j * cols : t * channels + (j + 1) * cols] for t in range(3)]
-        quads.append(outw_ref[...].astype(F32)[:, part])
-        S2[j] = jnp.concatenate([jnp.concatenate(quads, axis=1), zeros8b], axis=0).astype(BF16)
+        quads = [conv_ref[t].astype(F32)[:, part] for t in range(3)] + [outw[:, part]]
+        S1[j] = jnp.concatenate([jnp.concatenate(quads, axis=1), zeros4], axis=0).astype(BF16)
+        trio = [att[:, t * channels + j * cols : t * channels + (j + 1) * cols] for t in range(3)]
+        S2[j] = jnp.concatenate([jnp.concatenate(trio, axis=1), zeros3], axis=0).astype(BF16)
     pl.semaphore_wait(barrier, planes - 1 + dps - 1)
 
     def remote(src, dst, ss, rs, where):
@@ -177,13 +177,20 @@
         p = peer(j)
         return remote(src.at[p], dst.at[f], a_s.at[k, j], a_r.at[k, j], {"frame": p})
 
-    def lat_copy(j):
-        return remote(lat_ref, L.at[my_frames], lat_s.at[j], lat_r.at[j], {"frame": peer(j)})
+    side = [f + 1 - 2 * (f % 2), f + 2 - 4 * (f // 2)]
+    diag = planes - 1 - f
+
+    def lat_copy(n):
+        return remote(lat_ref, L.at[my_frames], lat_s.at[n], lat_r.at[n], {"frame": side[n]})
+
+    def lat_pass(n):
+        part = pl.ds(side[n] * mine + n * (mine // 2), mine // 2)
+        return remote(L.at[part], L.at[part], lat_s.at[2 + n], lat_r.at[2 + n], {"frame": side[1 - n]})
 
     for j in range(1, planes):
         a_copy(0, j).start()
-    for j in range(1, planes):
-        lat_copy(j).start()
+    for n in range(2):
+        lat_copy(n).start()
     for j in range(1, planes):
         a_copy(1, j).start()
     L[my_frames] = lat_ref[...]
@@ -200,13 +207,6 @@
 
     def guarded(cond, fn):
         pl.when(cond)(fn)
-
-    def push(k, owner, step, right, left, act):
-        if right is not None:
-            guarded(right, lambda: act(g_copy(k, owner, 3 * step, d + 2)))
-        if left is not None:
-            guarded(left, lambda: act(g_copy(k, owner, 3 * step + 1, d - 2)))
-        return None
 
     def steps_of(k, step, act):
         if step == 0:
@@ -260,12 +260,16 @@
     for j in range(1, planes):
         a_copy(1, j).wait_recv()
     GA[d] = stack(A2).astype(BF16)
-    for step in range(1, levels):
+    relay(0, 1)
+    for n in range(2):
+        lat_copy(n).wait_recv()
+        lat_pass(n).start()
+    for step in range(2, levels - 1):
         relay(0, step)
     relay(1, 0)
 
-    for j in range(1, planes):
-        lat_copy(j).wait_recv()
+    for n in range(2):
+        lat_pass(n).wait_recv()
 
     def fold(rows):
         return jnp.sum(rows.reshape(pixels // 8, 8, channels), axis=0)
@@ -292,47 +296,16 @@
         H[i] = (scaled / (1.0 + jnp.exp(-scaled))).astype(BF16)
         return carry
 
+    relay(0, levels - 1)
+    relay(1, 1)
     lax.fori_loop(0, frames, hide_frame, 0)
-    relay(1, 1)
 
     from_sibling(0)
     Y[0] = jnp.zeros(Y.shape[1:], F32)
     Y[frames + 1] = jnp.zeros(Y.shape[1:], F32)
 
-    def conv_pair(i, carry):
-        rows = H[pl.ds(2 * i, 2)].reshape(2 * pixels, channels)
-        weight = GC[:, 0:block, :].reshape(dps * block, 3 * cols)
-        y = jnp.dot(rows, weight, preferred_element_type=F32)
-        Y[pl.ds(2 * i + 1, 2)] = y.reshape(2, pixels, 3 * cols)
-        return carry
-
-    lax.fori_loop(0, frames // 2, conv_pair, 0)
-    times = GC[:, block : block + 16, :].reshape(dps * 16, 3 * cols)
-    tb = jnp.dot(feat_ref[...], times, preferred_element_type=F32)
-    bias = tb[0:1, 0:cols] + tb[1:2, cols : 2 * cols] + tb[2:3, 2 * cols : 3 * cols]
-
-    def res_frame(i, carry):
-        conv = Y[i][:, 0:cols] + Y[i + 1][:, cols : 2 * cols] + Y[i + 2][:, 2 * cols : 3 * cols]
-        x = L[i].astype(F32)
-        own = x[:, 0:cols]
-        for j in range(1, planes):
-            own = jnp.where(f == j, x[:, j * cols : (j + 1) * cols], own)
-        RS[f, i] = (own + (conv + bias)).astype(BF16)
-        return carry
-
-    lax.fori_loop(0, frames, res_frame, 0)
-
-    def rs_copy(j):
-        return remote(RS.at[f], RS.at[f], rs_s.at[j], rs_r.at[j], {"frame": peer(j)})
-
-    for j in range(1, planes):
-        rs_copy(j).start()
-    for step in range(2, levels):
-        relay(1, step)
-    from_sibling(1)
-
     half = dps * block // 2
-    WO[f] = GA[:, :, 3 * cols : 4 * cols].reshape(dps * block, cols)
+    WO[f] = GC[:, 0:block, 3 * cols : 4 * cols].reshape(dps * block, cols)
 
     def wo_copy(j):
         part = pl.ds(pl.multiple_of(c * half, 16), half)
@@ -340,41 +313,101 @@
 
     def wo_share(j):
         part = pl.ds(pl.multiple_of(c * half, 16), half)
-        s = source(j)
-        return remote(WO.at[s, part], WO.at[s, part], wf_s.at[j], wo_r.at[j, 1], {"dp": sib})
-
-    for j in range(1, planes):
-        rs_copy(j).wait_recv()
+        t = source(j)
+        return remote(WO.at[t, part], WO.at[t, part], wf_s.at[j], wo_r.at[j, 1], {"dp": sib})
+
     for j in range(1, planes):
         wo_copy(j).start()
 
-    def rows_of(i):
-        return jnp.concatenate([RS[j, i].astype(F32) for j in range(planes)], axis=1)
-
-    def norm_frame(i, carry):
-        rows = rows_of(i)
-        mean = jnp.mean(rows, axis=-1, keepdims=True)
-        dev = rows - mean
-        var = jnp.mean(dev * dev, axis=-1, keepdims=True)
-        H[i] = (dev / jnp.sqrt(var + 1e-05)).astype(BF16)
-        return carry
-
-    lax.fori_loop(0, frames, norm_frame, 0)
+    pairs = frames // 2
+
+    def conv_pair(i):
+        rows = H[2 * i : 2 * i + 2].reshape(2 * pixels, channels)
+        weight = GC[:, 0:block, 0 : 3 * cols].reshape(dps * block, 3 * cols)
+        y = jnp.dot(rows, weight, preferred_element_type=F32)
+        Y[2 * i + 1 : 2 * i + 3] = y.reshape(2, pixels, 3 * cols)
+
+    times = GC[:, block : block + 16, 0 : 3 * cols].reshape(dps * 16, 3 * cols)
+    tb = jnp.dot(feat_ref[...], times, preferred_element_type=F32)
+    bias = tb[0:1, 0:cols] + tb[1:2, cols : 2 * cols] + tb[2:3, 2 * cols : 3 * cols]
+
+    def res_pair(p):
+        both = []
+        for i in (2 * p, 2 * p + 1):
+            conv = Y[i][:, 0:cols] + Y[i + 1][:, cols : 2 * cols] + Y[i + 2][:, 2 * cols : 3 * cols]
+            x = L[i].astype(F32)
+            own = x[:, 0:cols]
+            for j in range(1, planes):
+                own = jnp.where(f == j, x[:, j * cols : (j + 1) * cols], own)
+            both.append(own + (conv + bias))
+        RS[f, p] = jnp.concatenate(both, axis=1).astype(BF16)
+
+    def rs_copy(p, n):
+        return remote(RS.at[f, p], RS.at[f, p], rs_s.at[p, n], rs_r.at[p, n], {"frame": side[n]})
+
+    def rs_pass(p, n):
+        part = pl.ds(n * (pixels // 2), pixels // 2)
+        piece = RS.at[side[n], p, part]
+        return remote(piece, piece, rs_s.at[p, 2 + n], rs_r.at[p, 2 + n], {"frame": side[1 - n]})
+
+    def send_pair(p):
+        res_pair(p)
+        for n in range(2):
+            rs_copy(p, n).start()
+
+    def pass_pair(p):
+        for n in range(2):
+            rs_copy(p, n).wait_recv()
+            rs_pass(p, n).start()
+
+    conv_pair(0)
+    for p in range(pairs):
+        if p + 1 < pairs:
+            conv_pair(p + 1)
+        send_pair(p)
+        if p == 0:
+            for step in range(2, levels):
+                relay(1, step)
+        else:
+            pass_pair(p - 1)
+    from_sibling(1)
+
+    def rows_of(p, n):
+        return jnp.concatenate(
+            [RS[j, p].astype(F32)[:, n * cols : (n + 1) * cols] for j in range(planes)], axis=1
+        )
+
+    def norm_pair(p):
+        for n in range(2):
+            rows = rows_of(p, n)
+            mean = jnp.mean(rows, axis=-1, keepdims=True)
+            dev = rows - mean
+            var = jnp.mean(dev * dev, axis=-1, keepdims=True)
+            H[2 * p + n] = (dev / jnp.sqrt(var + 1e-05)).astype(BF16)
+
     pad = jnp.zeros((pixels, HPAD - cols), F32)
 
-    def triple_pair(i, carry):
-        rows = H[pl.ds(2 * i, 2)].reshape(2 * pixels, channels)
+    def triple_pair(i):
+        rows = H[2 * i : 2 * i + 2].reshape(2 * pixels, channels)
         weight = GA[:, :, 0 : 3 * cols].reshape(dps * block, 3 * cols)
         y = jnp.dot(rows, weight, preferred_element_type=F32)
         for n in range(2):
             for t, buf in enumerate((Q, K, V)):
                 piece = y[n * pixels : (n + 1) * pixels, t * cols : (t + 1) * cols]
                 buf[2 * i + n] = jnp.concatenate([piece, pad], axis=1).astype(BF16)
-        return carry
-
-    lax.fori_loop(0, frames // 2, triple_pair, 0)
-
-    def attend(i, carry):
+
+    for p in range(pairs):
+        if p == 0:
+            pass_pair(pairs - 1)
+        for n in range(2):
+            rs_pass(p, n).wait_recv()
+        norm_pair(p)
+        triple_pair(p)
+    for j in range(1, planes):
+        wo_copy(j).wait_recv()
+        wo_share(j).start()
+
+    def attend(i):
         q = Q[i]
         prods = jnp.concatenate([q * K[g] for g in range(frames)], axis=1)
         scores = jnp.dot(prods, e_ref[...], preferred_element_type=F32) * (1.0 / math.sqrt(HD))
@@ -390,43 +423,48 @@
         acc = spreads[:, 0:HPAD] * V[0].astype(F32)
         for g in range(1, frames):
             acc = acc + spreads[:, g * HPAD : (g + 1) * HPAD] * V[g].astype(F32)
-        ATS[i] = acc[:, 0:cols].astype(BF16)
+        return acc[:, 0:cols]
+
+    def attend_pair(j, carry):
+        p = peer(j)
+        both = [attend(p * mine + n) for n in range(mine)]
+        ATS[p] = jnp.concatenate(both, axis=1).astype(BF16)
+        pl.when(j < planes)(lambda: at_copy(j).start())
         return carry
-
-    lax.fori_loop(0, frames, attend, 0)
 
     def at_copy(j):
         p = peer(j)
-        return remote(ATS.at[pl.ds(p * mine, mine)], AT.at[f], at_s.at[j], at_r.at[j], {"frame": p})
-
-    for j in range(1, planes):
-        at_copy(j).start()
-    AT[f] = ATS[my_frames]
-    for j in range(1, planes):
-        wo_copy(j).wait_recv()
-        wo_share(j).start()
+        return remote(ATS.at[p], AT.at[f], at_s.at[j], at_r.at[j], {"frame": p})
+
+    lax.fori_loop(1, planes + 1, attend_pair, 0)
+    AT[f] = ATS[f]
     for j in range(1, planes):
         wo_share(j).wait_recv()
     for j in range(1, planes):
         at_copy(j).wait_recv()
 
-    def out_frame(i, carry):
-        a = jnp.concatenate([AT[j, i].astype(F32) for j in range(planes)], axis=1).astype(BF16)
-        parts = [jnp.dot(a, WO[j], preferred_element_type=F32) for j in range(planes)]
-        mixed = rows_of(f * mine + i) + jnp.concatenate(parts, axis=1)
-        out_ref[i] = mixed.astype(BF16)
-        return carry
-
-    lax.fori_loop(0, mine, out_frame, 0)
+    wide = []
+    for n in range(mine):
+        heads = [AT[j].astype(F32)[:, n * cols : (n + 1) * cols] for j in range(planes)]
+        wide.append(jnp.concatenate(heads, axis=1).astype(BF16))
+    a = jnp.concatenate(wide, axis=0)
+    parts = [jnp.dot(a, WO[j], preferred_element_type=F32) for j in range(planes)]
+    mixed = jnp.concatenate(parts, axis=1)
+    for n in range(mine):
+        out_ref[n] = (rows_of(f, n) + mixed[n * pixels : (n + 1) * pixels]).astype(BF16)
 
     for j in range(1, planes):
         a_copy(0, j).wait_send()
         a_copy(1, j).wait_send()
-        lat_copy(j).wait_send()
-        rs_copy(j).wait_send()
         wo_copy(j).wait_send()
         wo_share(j).wait_send()
         at_copy(j).wait_send()
+    for n in range(2):
+        lat_copy(n).wait_send()
+        lat_pass(n).wait_send()
+        for p in range(pairs):
+            rs_copy(p, n).wait_send()
+            rs_pass(p, n).wait_send()
     drain(0)
     drain(1)
 
@@ -457,7 +495,7 @@
     feats = jnp.pad(features.transpose(1, 0, 2).reshape(3, dps * 16), ((0, 13), (0, 0)))
     times = lax.dynamic_slice_in_dim(time_weight, f * cols, cols, axis=1)
     times = jnp.pad(times, ((0, 48 - rows), (0, 0))).reshape(3, 16, cols)
-    times = times.transpose(1, 0, 2).reshape(16, 3 * cols)
+    times = jnp.pad(times.transpose(1, 0, 2).reshape(16, 3 * cols), ((0, 0), (0, cols)))
     ind, indb, e, et = indicators(frames, channels, cols)
     vmem = pl.BlockSpec(memory_space=pltpu.VMEM)
     DMA = pltpu.SemaphoreType.DMA
@@ -470,24 +508,24 @@
         scratch_shapes=[
             pltpu.VMEM((frames, pixels, channels), BF16),
             pltpu.VMEM((frames, pixels, channels), BF16),
+            pltpu.VMEM((planes, depth + 8, 4 * cols), BF16),
             pltpu.VMEM((planes, depth + 8, 3 * cols), BF16),
             pltpu.VMEM((planes, depth + 8, 4 * cols), BF16),
             pltpu.VMEM((planes, depth + 8, 3 * cols), BF16),
-            pltpu.VMEM((planes, depth + 8, 4 * cols), BF16),
-            pltpu.VMEM((dps, block + 16, 3 * cols), BF16),
-            pltpu.VMEM((dps, block, 4 * cols), BF16),
+            pltpu.VMEM((dps, block + 16, 4 * cols), BF16),
+            pltpu.VMEM((dps, block, 3 * cols), BF16),
             pltpu.VMEM((frames + 2, pixels, 3 * cols), F32),
-            pltpu.VMEM((planes, frames, pixels, cols), BF16),
+            pltpu.VMEM((planes, frames // 2, pixels, 2 * cols), BF16),
             pltpu.VMEM((frames, pixels, HPAD), BF16),
             pltpu.VMEM((frames, pixels, HPAD), BF16),
             pltpu.VMEM((frames, pixels, HPAD), BF16),
-            pltpu.VMEM((frames, pixels, cols), BF16),
-            pltpu.VMEM((planes, mine, pixels, cols), BF16),
+            pltpu.VMEM((planes, pixels, 2 * cols), BF16),
+            pltpu.VMEM((planes, pixels, 2 * cols), BF16),
             pltpu.VMEM((planes, dps * block, cols), BF16),
-            DMA((planes,)), DMA((planes,)),
+            DMA((4,)), DMA((4,)),
             DMA((2, planes)), DMA((2, planes)),
             DMA((2, slots)), DMA((2, dps)),
-            DMA((planes,)), DMA((planes,)),
+            DMA((frames // 2, 4)), DMA((frames // 2, 4)),
             DMA((planes,)), DMA((planes,)),
             DMA((planes,)), DMA((planes, 2)), DMA((planes,)),
         ],

time: 154 us -> 130 us (0.84)
  Pallas kernels: 148 us -> 124 us
    pallas_call x1, Pallas kernels: 148 us -> 124 us  [fast_shards(): pl.pallas_call(functools.partial(kernel, planes, dps), out_shape=jax.Shap...]
where the time goes in v2:
time: 130 us
  Pallas kernels  124 us (95%)
  local copies, waits for them, and re-layouts  4.7 us (4%)
    pallas_call x1, Pallas kernels, fast_shards(): pl.pallas_call(functools.partial(kernel, planes, dps), out_shape=jax.Shap...  124 us

profile of v2, /device:TPU:0, one launch (start us, length us, event | category | flops | bytes accessed | tf_op | source)
XLA Modules:
  0.0 129.7 jit_solution(7021032907650299576)
XLA Ops:
  0.0 0.0 copy-start
  0.7 0.0 copy-start.1
  0.7 0.1 sine_convert_fusion
  0.8 0.1 maximum_reduce_fusion
  0.9 0.1 convert_element_type.19
  1.0 0.4 copy-done.1
  1.4 0.6 broadcast_in_dim.8.gain_ref
  2.0 0.1 reshape.42
  2.1 0.1 reshape.43
  2.2 0.6 pad.17.feat_ref
  2.8 0.0 copy-done
  2.8 0.1 constant_dynamic-slice_fusion
  2.9 0.1 reshape.45
  3.0 0.6 pad.19.time_ref
  3.6 124.1 %shard_map.109 = bf16[2,128,1280]{2,1,0:T(8,128)(2,1)} custom-call(bf16[2,128,1280]{2,1,0:T(8,128)(2,1)} %bitcast.12, bf16[16,128]{1,0:T(8,128)(2,1)} %pad.17.feat_ref, f32[1,1280]{1,0:T(1,128)} %broadcast_in_dim.8.gain_ref, bf16[16,1280]{1,0:T(8,128)(2,1)} %pad.19.time_ref, bf16[3,40,1280]{2,1,0:T(8,128)(2,1)} %conv_ref.1, bf16[40,3840]{1,0:T(8,128)(2,1)} %att_ref.1, ...), custom_call_target="tpu_custom_call" | custom-call | flops 7000000000 | bytes 8000000 | tf_op jit(solution)/shard_map/pallas_call | solution.py:503
  127.7 2.0 %copy.19 = bf16[1,2,128,1280]{3,2,1,0:T(8,128)(2,1)} copy(bf16[1,2,128,1280]{3,2,1,0:T(8,128)(2,1)} %bitcast.8) | data formatting | bytes 1310720
  (4 shorter events, 0.0 us)
Async XLA Ops:
  0.0 2.8 %copy-start = (bf16[40,1280]{1,0:T(8,128)(2,1)S(1)}, bf16[40,1280]{1,0:T(8,128)(2,1)}, u32[]{:S(2)}) copy-start(bf16[40,1280]{1,0:T(8,128)(2,1)} %param.14) | copy-start | bytes 307204
  0.7 0.7 copy-start.1

commit v3 on v2

--- a/solution.py
+++ b/solution.py
@@ -152,10 +152,11 @@
     outw = outw_ref[...].astype(F32)
     for j in range(planes):
         part = slice(j * cols, (j + 1) * cols)
-        quads = [conv_ref[t].astype(F32)[:, part] for t in range(3)] + [outw[:, part]]
-        S1[j] = jnp.concatenate([jnp.concatenate(quads, axis=1), zeros4], axis=0).astype(BF16)
-        trio = [att[:, t * channels + j * cols : t * channels + (j + 1) * cols] for t in range(3)]
-        S2[j] = jnp.concatenate([jnp.concatenate(trio, axis=1), zeros3], axis=0).astype(BF16)
+        taps = [conv_ref[t].astype(F32)[:, part] for t in range(3)]
+        S1[j] = jnp.concatenate([jnp.concatenate(taps, axis=1), zeros3], axis=0).astype(BF16)
+        quads = [att[:, t * channels + j * cols : t * channels + (j + 1) * cols] for t in range(3)]
+        quads.append(outw[:, part])
+        S2[j] = jnp.concatenate([jnp.concatenate(quads, axis=1), zeros4], axis=0).astype(BF16)
     pl.semaphore_wait(barrier, planes - 1 + dps - 1)
 
     def remote(src, dst, ss, rs, where):
@@ -303,21 +304,6 @@
     from_sibling(0)
     Y[0] = jnp.zeros(Y.shape[1:], F32)
     Y[frames + 1] = jnp.zeros(Y.shape[1:], F32)
-
-    half = dps * block // 2
-    WO[f] = GC[:, 0:block, 3 * cols : 4 * cols].reshape(dps * block, cols)
-
-    def wo_copy(j):
-        part = pl.ds(pl.multiple_of(c * half, 16), half)
-        return remote(WO.at[f, part], WO.at[f, part], wo_s.at[j], wo_r.at[j, 0], {"frame": peer(j)})
-
-    def wo_share(j):
-        part = pl.ds(pl.multiple_of(c * half, 16), half)
-        t = source(j)
-        return remote(WO.at[t, part], WO.at[t, part], wf_s.at[j], wo_r.at[j, 1], {"dp": sib})
-
-    for j in range(1, planes):
-        wo_copy(j).start()
 
     pairs = frames // 2
 
@@ -365,12 +351,6 @@
         if p + 1 < pairs:
             conv_pair(p + 1)
         send_pair(p)
-        if p == 0:
-            for step in range(2, levels):
-                relay(1, step)
-        else:
-            pass_pair(p - 1)
-    from_sibling(1)
 
     def rows_of(p, n):
         return jnp.concatenate(
@@ -396,20 +376,48 @@
                 piece = y[n * pixels : (n + 1) * pixels, t * cols : (t + 1) * cols]
                 buf[2 * i + n] = jnp.concatenate([piece, pad], axis=1).astype(BF16)
 
-    for p in range(pairs):
-        if p == 0:
-            pass_pair(pairs - 1)
+    def arrive_pair(p):
         for n in range(2):
             rs_pass(p, n).wait_recv()
         norm_pair(p)
+
+    waits = levels - 2
+    for p in range(pairs):
+        pass_pair(p)
+        if p > 0:
+            arrive_pair(p - 1)
+        if p % 2 == 1 and p // 2 < waits:
+            relay(1, 2 + p // 2)
+    for step in range(2 + pairs // 2, levels):
+        relay(1, step)
+    from_sibling(1)
+
+    half = dps * block // 2
+    own_w = GA[:, :, 3 * cols : 4 * cols].reshape(dps * block, cols).astype(F32)
+    WO[f] = jnp.concatenate([own_w[0:half], own_w[half : 2 * half]], axis=1).astype(BF16)
+    quarter = half // 2
+    wo_part = pl.ds(pl.multiple_of(c * quarter, 16), quarter)
+
+    def wo_copy(j):
+        piece = WO.at[f, wo_part]
+        return remote(piece, piece, wo_s.at[j], wo_r.at[j, 0], {"frame": peer(j)})
+
+    def wo_share(j):
+        piece = WO.at[source(j), wo_part]
+        return remote(piece, piece, wf_s.at[j], wo_r.at[j, 1], {"dp": sib})
+
+    for j in range(1, planes):
+        wo_copy(j).start()
+    arrive_pair(pairs - 1)
+    for p in range(pairs):
         triple_pair(p)
-    for j in range(1, planes):
-        wo_copy(j).wait_recv()
-        wo_share(j).start()
-
-    def attend(i):
-        q = Q[i]
-        prods = jnp.concatenate([q * K[g] for g in range(frames)], axis=1)
+
+    def attend(p):
+        prods = []
+        for n in range(mine):
+            q = Q[p * mine + n]
+            prods.append(jnp.concatenate([q * K[g] for g in range(frames)], axis=1))
+        prods = jnp.concatenate(prods, axis=0)
         scores = jnp.dot(prods, e_ref[...], preferred_element_type=F32) * (1.0 / math.sqrt(HD))
         peak = scores
         for shift in (8, 16, 32):
@@ -419,16 +427,18 @@
         for shift in (8, 16, 32):
             total = total + pltpu.roll(total, shift, 1)
         probs = (expo / total).astype(BF16)
-        spreads = jnp.dot(probs, et_ref[...], preferred_element_type=F32)
-        acc = spreads[:, 0:HPAD] * V[0].astype(F32)
-        for g in range(1, frames):
-            acc = acc + spreads[:, g * HPAD : (g + 1) * HPAD] * V[g].astype(F32)
-        return acc[:, 0:cols]
+        acc = [0.0] * mine
+        for g in range(frames):
+            lanes = slice(g * HPAD, (g + 1) * HPAD)
+            spreads = jnp.dot(probs, et_ref[:, lanes], preferred_element_type=F32)
+            v = V[g].astype(F32)
+            for n in range(mine):
+                acc[n] = acc[n] + spreads[n * pixels : (n + 1) * pixels] * v
+        return jnp.concatenate([part[:, 0:cols] for part in acc], axis=1)
 
     def attend_pair(j, carry):
         p = peer(j)
-        both = [attend(p * mine + n) for n in range(mine)]
-        ATS[p] = jnp.concatenate(both, axis=1).astype(BF16)
+        ATS[p] = attend(p).astype(BF16)
         pl.when(j < planes)(lambda: at_copy(j).start())
         return carry
 
@@ -438,6 +448,9 @@
 
     lax.fori_loop(1, planes + 1, attend_pair, 0)
     AT[f] = ATS[f]
+    for j in range(1, planes):
+        wo_copy(j).wait_recv()
+        wo_share(j).start()
     for j in range(1, planes):
         wo_share(j).wait_recv()
     for j in range(1, planes):
@@ -448,7 +461,11 @@
         heads = [AT[j].astype(F32)[:, n * cols : (n + 1) * cols] for j in range(planes)]
         wide.append(jnp.concatenate(heads, axis=1).astype(BF16))
     a = jnp.concatenate(wide, axis=0)
-    parts = [jnp.dot(a, WO[j], preferred_element_type=F32) for j in range(planes)]
+    parts = []
+    for j in range(planes):
+        left, right = WO[j][:, 0:cols], WO[j][:, cols : 2 * cols]
+        part = jnp.dot(a[:, 0:half], left, preferred_element_type=F32)
+        parts.append(part + jnp.dot(a[:, half : 2 * half], right, preferred_element_type=F32))
     mixed = jnp.concatenate(parts, axis=1)
     for n in range(mine):
         out_ref[n] = (rows_of(f, n) + mixed[n * pixels : (n + 1) * pixels]).astype(BF16)
@@ -495,7 +512,7 @@
     feats = jnp.pad(features.transpose(1, 0, 2).reshape(3, dps * 16), ((0, 13), (0, 0)))
     times = lax.dynamic_slice_in_dim(time_weight, f * cols, cols, axis=1)
     times = jnp.pad(times, ((0, 48 - rows), (0, 0))).reshape(3, 16, cols)
-    times = jnp.pad(times.transpose(1, 0, 2).reshape(16, 3 * cols), ((0, 0), (0, cols)))
+    times = times.transpose(1, 0, 2).reshape(16, 3 * cols)
     ind, indb, e, et = indicators(frames, channels, cols)
     vmem = pl.BlockSpec(memory_space=pltpu.VMEM)
     DMA = pltpu.SemaphoreType.DMA
@@ -508,12 +525,12 @@
         scratch_shapes=[
             pltpu.VMEM((frames, pixels, channels), BF16),
             pltpu.VMEM((frames, pixels, channels), BF16),
+            pltpu.VMEM((planes, depth + 8, 3 * cols), BF16),
             pltpu.VMEM((planes, depth + 8, 4 * cols), BF16),
             pltpu.VMEM((planes, depth + 8, 3 * cols), BF16),
             pltpu.VMEM((planes, depth + 8, 4 * cols), BF16),
-            pltpu.VMEM((planes, depth + 8, 3 * cols), BF16),
-            pltpu.VMEM((dps, block + 16, 4 * cols), BF16),
-            pltpu.VMEM((dps, block, 3 * cols), BF16),
+            pltpu.VMEM((dps, block + 16, 3 * cols), BF16),
+            pltpu.VMEM((dps, block, 4 * cols), BF16),
             pltpu.VMEM((frames + 2, pixels, 3 * cols), F32),
             pltpu.VMEM((planes, frames // 2, pixels, 2 * cols), BF16),
             pltpu.VMEM((frames, pixels, HPAD), BF16),
@@ -521,7 +538,7 @@
             pltpu.VMEM((frames, pixels, HPAD), BF16),
             pltpu.VMEM((planes, pixels, 2 * cols), BF16),
             pltpu.VMEM((planes, pixels, 2 * cols), BF16),
-            pltpu.VMEM((planes, dps * block, cols), BF16),
+            pltpu.VMEM((planes, dps * block // 2, 2 * cols), BF16),
             DMA((4,)), DMA((4,)),
             DMA((2, planes)), DMA((2, planes)),
             DMA((2, slots)), DMA((2, dps)),

time: 130 us -> 123 us (0.946)
  Pallas kernels: 124 us -> 117 us
    pallas_call x1, Pallas kernels: 124 us -> 117 us  [fast_shards(): pl.pallas_call(functools.partial(kernel, planes, dps), out_shape=jax.Shap...]
where the time goes in v3:
time: 123 us
  Pallas kernels  117 us (95%)
  local copies, waits for them, and re-layouts  4.69 us (4%)
    pallas_call x1, Pallas kernels, fast_shards(): pl.pallas_call(functools.partial(kernel, planes, dps), out_shape=jax.Shap...  117 us

profile of v3, /device:TPU:0, one launch (start us, length us, event | category | flops | bytes accessed | tf_op | source)
XLA Modules:
  0.0 122.9 jit_solution(11139328297982494458)
XLA Ops:
  0.0 0.0 copy-start
  0.7 0.0 copy-start.1
  0.7 0.1 sine_convert_fusion
  0.8 0.1 maximum_reduce_fusion
  0.9 0.1 convert_element_type.17
  1.0 0.4 copy-done.1
  1.4 0.6 broadcast_in_dim.8.gain_ref
  2.0 0.1 reshape.42
  2.1 0.1 reshape.43
  2.2 0.6 pad.13.feat_ref
  2.8 0.0 copy-done
  2.8 0.1 constant_dynamic-slice_fusion
  2.9 0.7 reshape.45.time_ref
  3.6 117.3 %shard_map.109 = bf16[2,128,1280]{2,1,0:T(8,128)(2,1)} custom-call(bf16[2,128,1280]{2,1,0:T(8,128)(2,1)} %bitcast.12, bf16[16,128]{1,0:T(8,128)(2,1)} %pad.13.feat_ref, f32[1,1280]{1,0:T(1,128)} %broadcast_in_dim.8.gain_ref, bf16[16,960]{1,0:T(8,128)(2,1)} %reshape.45.time_ref, bf16[3,40,1280]{2,1,0:T(8,128)(2,1)} %conv_ref.1, bf16[40,3840]{1,0:T(8,128)(2,1)} %att_ref.1, ...), custom_call_target="tpu_custom_call" | custom-call | flops 7000000000 | bytes 8000000 | tf_op jit(solution)/shard_map/pallas_call | solution.py:520
  120.9 2.0 %copy.19 = bf16[1,2,128,1280]{3,2,1,0:T(8,128)(2,1)} copy(bf16[1,2,128,1280]{3,2,1,0:T(8,128)(2,1)} %bitcast.8) | data formatting | bytes 1310720
  (4 shorter events, 0.0 us)
Async XLA Ops:
  0.0 2.8 %copy-start = (bf16[40,1280]{1,0:T(8,128)(2,1)S(1)}, bf16[40,1280]{1,0:T(8,128)(2,1)}, u32[]{:S(2)}) copy-start(bf16[40,1280]{1,0:T(8,128)(2,1)} %param.14) | copy-start | bytes 307204
  0.7 0.7 copy-start.1

commit v4 on v3

--- a/solution.py
+++ b/solution.py
@@ -123,7 +123,7 @@
 
 
 def kernel(
-    planes, dps, lat_ref, feat_ref, gain_ref, time_ref, conv_ref, att_ref, outw_ref,
+    planes, dps, lat_ref, step_ref, wave_ref, gain_ref, time_ref, conv_ref, att_ref, outw_ref,
     ind_ref, indb_ref, e_ref, et_ref, out_ref,
     L, H, S1, S2, A1, A2, GC, GA, Y, RS, Q, K, V, ATS, AT, WO,
     lat_s, lat_r, a_s, a_r, g_s, g_r, rs_s, rs_r, at_s, at_r, wo_s, wo_r, wf_s,
@@ -256,17 +256,23 @@
     for j in range(1, planes):
         a_copy(0, j).wait_recv()
     GC[d, 0:block] = stack(A1).astype(BF16)
-    GC[d, block : block + 16] = time_ref[...]
+    times_all = time_ref[...].astype(F32)
+    own_t = times_all[:, 0:cols]
+    for j in range(1, planes):
+        own_t = jnp.where(f == j, times_all[:, j * cols : (j + 1) * cols], own_t)
+    own_t = jnp.concatenate([own_t, jnp.zeros((48 - own_t.shape[0], cols), F32)], axis=0)
+    own_t = jnp.concatenate([own_t[16 * n : 16 * n + 16] for n in range(3)], axis=1)
+    GC[d, block : block + 16] = own_t.astype(BF16)
     relay(0, 0)
-    for j in range(1, planes):
-        a_copy(1, j).wait_recv()
-    GA[d] = stack(A2).astype(BF16)
     relay(0, 1)
     for n in range(2):
         lat_copy(n).wait_recv()
         lat_pass(n).start()
     for step in range(2, levels - 1):
         relay(0, step)
+    for j in range(1, planes):
+        a_copy(1, j).wait_recv()
+    GA[d] = stack(A2).astype(BF16)
     relay(1, 0)
 
     for n in range(2):
@@ -290,7 +296,7 @@
 
     total2 = lax.fori_loop(0, frames, dev_frame, start)
     spread = group_mean(jnp.sum(total2, axis=0, keepdims=True), ind, indb, count)
-    scale = gain_ref[...] / jnp.sqrt(spread + 1e-05)
+    scale = gain_ref[...].reshape(1, channels) / jnp.sqrt(spread + 1e-05)
 
     def hide_frame(i, carry):
         scaled = (L[i].astype(F32) - center) * scale
@@ -307,14 +313,19 @@
 
     pairs = frames // 2
 
-    def conv_pair(i):
-        rows = H[2 * i : 2 * i + 2].reshape(2 * pixels, channels)
+    quad = 4
+
+    def conv_quad(i):
+        rows = H[quad * i : quad * (i + 1)].reshape(quad * pixels, channels)
         weight = GC[:, 0:block, 0 : 3 * cols].reshape(dps * block, 3 * cols)
         y = jnp.dot(rows, weight, preferred_element_type=F32)
-        Y[2 * i + 1 : 2 * i + 3] = y.reshape(2, pixels, 3 * cols)
+        Y[quad * i + 1 : quad * (i + 1) + 1] = y.reshape(quad, pixels, 3 * cols)
 
     times = GC[:, block : block + 16, 0 : 3 * cols].reshape(dps * 16, 3 * cols)
-    tb = jnp.dot(feat_ref[...], times, preferred_element_type=F32)
+    angles = step_ref[0].astype(F32) * wave_ref[0]
+    which = wave_ref[1]
+    feats = jnp.where(which == 1.0, jnp.cos(angles), jnp.where(which == 2.0, jnp.sin(angles), 0.0))
+    tb = jnp.dot(feats.astype(BF16), times, preferred_element_type=F32)
     bias = tb[0:1, 0:cols] + tb[1:2, cols : 2 * cols] + tb[2:3, 2 * cols : 3 * cols]
 
     def res_pair(p):
@@ -346,10 +357,10 @@
             rs_copy(p, n).wait_recv()
             rs_pass(p, n).start()
 
-    conv_pair(0)
+    conv_quad(0)
     for p in range(pairs):
-        if p + 1 < pairs:
-            conv_pair(p + 1)
+        if p % 2 == 1 and p + 1 < pairs:
+            conv_quad((p + 1) // 2)
         send_pair(p)
 
     def rows_of(p, n):
@@ -367,14 +378,14 @@
 
     pad = jnp.zeros((pixels, HPAD - cols), F32)
 
-    def triple_pair(i):
-        rows = H[2 * i : 2 * i + 2].reshape(2 * pixels, channels)
+    def triple_quad(i):
+        rows = H[quad * i : quad * (i + 1)].reshape(quad * pixels, channels)
         weight = GA[:, :, 0 : 3 * cols].reshape(dps * block, 3 * cols)
         y = jnp.dot(rows, weight, preferred_element_type=F32)
-        for n in range(2):
+        for n in range(quad):
             for t, buf in enumerate((Q, K, V)):
                 piece = y[n * pixels : (n + 1) * pixels, t * cols : (t + 1) * cols]
-                buf[2 * i + n] = jnp.concatenate([piece, pad], axis=1).astype(BF16)
+                buf[quad * i + n] = jnp.concatenate([piece, pad], axis=1).astype(BF16)
 
     def arrive_pair(p):
         for n in range(2):
@@ -409,8 +420,8 @@
     for j in range(1, planes):
         wo_copy(j).start()
     arrive_pair(pairs - 1)
-    for p in range(pairs):
-        triple_pair(p)
+    for i in range(frames // quad):
+        triple_quad(i)
 
     def attend(p):
         prods = []
@@ -436,8 +447,14 @@
                 acc[n] = acc[n] + spreads[n * pixels : (n + 1) * pixels] * v
         return jnp.concatenate([part[:, 0:cols] for part in acc], axis=1)
 
+    def share_weight():
+        for n in range(1, planes):
+            wo_copy(n).wait_recv()
+            wo_share(n).start()
+
     def attend_pair(j, carry):
         p = peer(j)
+        pl.when(j == planes)(share_weight)
         ATS[p] = attend(p).astype(BF16)
         pl.when(j < planes)(lambda: at_copy(j).start())
         return carry
@@ -448,9 +465,6 @@
 
     lax.fori_loop(1, planes + 1, attend_pair, 0)
     AT[f] = ATS[f]
-    for j in range(1, planes):
-        wo_copy(j).wait_recv()
-        wo_share(j).start()
     for j in range(1, planes):
         wo_share(j).wait_recv()
     for j in range(1, planes):
@@ -505,14 +519,15 @@
     cols = channels // planes
     depth = conv_weight.shape[1]
     block = depth * planes
-    f = lax.axis_index("frame")
     rows = time_weight.shape[0]
-    features = sinusoid(timestep).astype(BF16).reshape(dps, rows)
-    features = jnp.pad(features, ((0, 0), (0, 48 - rows))).reshape(dps, 3, 16)
-    feats = jnp.pad(features.transpose(1, 0, 2).reshape(3, dps * 16), ((0, 13), (0, 0)))
-    times = lax.dynamic_slice_in_dim(time_weight, f * cols, cols, axis=1)
-    times = jnp.pad(times, ((0, 48 - rows), (0, 0))).reshape(3, 16, cols)
-    times = times.transpose(1, 0, 2).reshape(16, 3 * cols)
+    lane, line = np.arange(dps * 16)[None, :], np.arange(16)[:, None]
+    inside = 16 * line + lane % 16
+    entry = rows * (lane // 16) + inside
+    half_dim = TEMB // 2
+    ladder = (entry % half_dim).astype(np.float32)
+    freqs = np.exp(np.float32(-math.log(10000.0)) * ladder / np.float32(half_dim))
+    which = np.where(inside < rows, 1.0 + (entry >= half_dim), 0.0)
+    wave = jnp.asarray(np.stack([freqs, which]), F32)
     ind, indb, e, et = indicators(frames, channels, cols)
     vmem = pl.BlockSpec(memory_space=pltpu.VMEM)
     DMA = pltpu.SemaphoreType.DMA
@@ -520,7 +535,7 @@
     out = pl.pallas_call(
         functools.partial(kernel, planes, dps),
         out_shape=jax.ShapeDtypeStruct((mine, pixels, channels), BF16),
-        in_specs=[vmem] * 11,
+        in_specs=[vmem, pl.BlockSpec(memory_space=pltpu.SMEM)] + [vmem] * 10,
         out_specs=vmem,
         scratch_shapes=[
             pltpu.VMEM((frames, pixels, channels), BF16),
@@ -551,7 +566,7 @@
         ),
         cost_estimate=pl.CostEstimate(flops=7_000_000_000, bytes_accessed=8_000_000, transcendentals=3_000_000),
     )(
-        latents[0], feats, norm_gain[None, :], times, conv_weight, attend_weight, output_weight,
+        latents[0], timestep, wave, norm_gain, time_weight, conv_weight, attend_weight, output_weight,
         ind, indb, e, et,
     )
     return out[None]

time: 123 us -> 109 us (0.89)
  Pallas kernels: 117 us -> 106 us
  local copies, waits for them, and re-layouts: 4.69 us -> 1.97 us
    pallas_call x1, Pallas kernels: 117 us -> 106 us  [fast_shards(): pl.pallas_call(functools.partial(kernel, planes, dps), out_shape=jax.Shap...]
where the time goes in v4:
time: 109 us
  Pallas kernels  106 us (97%)
  local copies, waits for them, and re-layouts  1.97 us (2%)
    pallas_call x1, Pallas kernels, fast_shards(): pl.pallas_call(functools.partial(kernel, planes, dps), out_shape=jax.Shap...  106 us

profile of v4, /device:TPU:0, one launch (start us, length us, event | category | flops | bytes accessed | tf_op | source)
XLA Modules:
  0.0 108.7 jit_solution(12375718854034952840)
XLA Ops:
  0.7 106.0 %shard_map.118 = bf16[2,128,1280]{2,1,0:T(8,128)(2,1)} custom-call(bf16[2,128,1280]{2,1,0:T(8,128)(2,1)} %bitcast.3, s32[1]{0:T(128)S(6)} %copy.14.step_ref, f32[2,16,128]{2,1,0:T(8,128)} %constant.10.clone.wave_ref, f32[1280]{0:T(1024)} %gain_ref.1, bf16[40,1280]{1,0:T(8,128)(2,1)} %time_ref.1, bf16[3,40,1280]{2,1,0:T(8,128)(2,1)} %conv_ref.1, ...), custom_call_target="tpu_custom_call" | custom-call | flops 7000000000 | bytes 8000000 | tf_op jit(solution)/shard_map/pallas_call | solution.py:535
  106.7 2.0 %copy.15 = bf16[1,2,128,1280]{3,2,1,0:T(8,128)(2,1)} copy(bf16[1,2,128,1280]{3,2,1,0:T(8,128)(2,1)} %bitcast.2) | data formatting | bytes 1310720

commit v5 on v4

--- a/solution.py
+++ b/solution.py
@@ -201,10 +201,13 @@
     def stack(buf):
         return jnp.concatenate([buf[j].astype(F32)[:depth] for j in range(planes)], axis=0)
 
-    G = (GC, GA)
+    cut = block // 2
+    G = ((GC, 0, cut), (GC, cut, cut + 16), (GA, 0, cut), (GA, cut, cut))
 
     def g_copy(k, owner, slot, target):
-        return remote(G[k].at[owner], G[k].at[owner], g_s.at[k, slot], g_r.at[k, owner], {"dp": target})
+        buf, first, size = G[k]
+        piece = buf.at[owner, pl.ds(first, size)]
+        return remote(piece, piece, g_s.at[k, slot], g_r.at[k, owner], {"dp": target})
 
     def guarded(cond, fn):
         pl.when(cond)(fn)
@@ -231,7 +234,11 @@
             guarded(z > 0, lambda: act(0, above, base + 2, d - 2))
             act(0, above, base + 3, sib)
 
-    def relay(k, step):
+    def relay(which, step):
+        relay_half(2 * which, step)
+        relay_half(2 * which + 1, step)
+
+    def relay_half(k, step):
         def act(kind, owner, slot, target):
             copy = g_copy(k, owner, slot, target)
             if kind == 1:
@@ -249,9 +256,10 @@
         for step in range(levels):
             steps_of(k, step, act)
 
-    def from_sibling(k):
-        for zz in range(levels):
-            g_copy(k, 2 * zz + 1 - c, 0, sib).wait_recv()
+    def from_sibling(which):
+        for k in (2 * which, 2 * which + 1):
+            for zz in range(levels):
+                g_copy(k, 2 * zz + 1 - c, 0, sib).wait_recv()
 
     for j in range(1, planes):
         a_copy(0, j).wait_recv()
@@ -496,8 +504,8 @@
         for p in range(pairs):
             rs_copy(p, n).wait_send()
             rs_pass(p, n).wait_send()
-    drain(0)
-    drain(1)
+    for k in range(4):
+        drain(k)
 
 
 def indicators(frames, channels, cols):
@@ -556,7 +564,7 @@
             pltpu.VMEM((planes, dps * block // 2, 2 * cols), BF16),
             DMA((4,)), DMA((4,)),
             DMA((2, planes)), DMA((2, planes)),
-            DMA((2, slots)), DMA((2, dps)),
+            DMA((4, slots)), DMA((4, dps)),
             DMA((frames // 2, 4)), DMA((frames // 2, 4)),
             DMA((planes,)), DMA((planes,)),
             DMA((planes,)), DMA((planes, 2)), DMA((planes,)),

time: 109 us -> 109 us (level)
  no operation moved by 1% of the time
where the time goes in v5:
time: 109 us
  Pallas kernels  106 us (97%)
  local copies, waits for them, and re-layouts  1.97 us (2%)
    pallas_call x1, Pallas kernels, fast_shards(): pl.pallas_call(functools.partial(kernel, planes, dps), out_shape=jax.Shap...  106 us

profile of v5, /device:TPU:0, one launch (start us, length us, event | category | flops | bytes accessed | tf_op | source)
XLA Modules:
  0.0 108.7 jit_solution(15569498146336988760)
XLA Ops:
  0.7 106.1 %shard_map.118 = bf16[2,128,1280]{2,1,0:T(8,128)(2,1)} custom-call(bf16[2,128,1280]{2,1,0:T(8,128)(2,1)} %bitcast.3, s32[1]{0:T(128)S(6)} %copy.14.step_ref, f32[2,16,128]{2,1,0:T(8,128)} %constant.10.clone.wave_ref, f32[1280]{0:T(1024)} %gain_ref.1, bf16[40,1280]{1,0:T(8,128)(2,1)} %time_ref.1, bf16[3,40,1280]{2,1,0:T(8,128)(2,1)} %conv_ref.1, ...), custom_call_target="tpu_custom_call" | custom-call | flops 7000000000 | bytes 8000000 | tf_op jit(solution)/shard_map/pallas_call | solution.py:543
  106.8 2.0 %copy.15 = bf16[1,2,128,1280]{3,2,1,0:T(8,128)(2,1)} copy(bf16[1,2,128,1280]{3,2,1,0:T(8,128)(2,1)} %bitcast.2) | data formatting | bytes 1310720
